TPU v7x, 256 devices: a whole 4x4x8 slice. The times are simulated.
256 devices in a mesh: grp: 16 (over y, x_hi, core), sh: 16 (over z, x_lo).
Axes of the slice: x: 4 (x_hi: 2, x_lo: 2; x = x_hi * 2 + x_lo), y: 4, z: 8, core: 2. Of those that a mesh axis runs over, the one named last changes fastest.
Arguments:
- factors: bfloat16 [48, 128, 14336], P('grp', None, 'sh'), may hold values from -0.5 to 0.5
- screen: int32 [48, 1, 112], P('grp', None, 'sh'), may hold values 0 or 1
- occ_energy: float32 [48], replicated, may hold values from -1.5 to -0.3
- virt_energy: float32 [128], replicated, may hold values from 0.5 to 3
Outputs:
- gamma: bfloat16 [48, 128, 14336], P('grp', 'sh')
Inputs may be any that keep to these rules, and one draw needn't show every extreme that they name: `screen`: 1 keeps a block of 128 virtual by 128 auxiliary functions of one occupied orbital, 0 screens it out.
All inputs are finite; a program needn't handle non-finite values.
Results may differ from a plain program's by a relative error of at most 0.0049.
Values may be sent and summed in bfloat16 or wider, within the bound.
No kernel may reach another device: no remote copies, remote signals or barrier semaphores. Data moves between devices by JAX's collectives and lax.ppermute only.
A program may use at most 64 MiB of HBM per device.

v0:
```python
import jax
import jax.numpy as jnp
from jax import lax
from jax.sharding import PartitionSpec as P

BLK = 128


def passed_along(value, axis, steps):
    count = lax.axis_size(axis)
    pairs = [(source, (source + steps) % count) for source in range(count)]
    return lax.ppermute(value, axis, pairs)


def on_device(factors, screen, occ_energy, virt_energy):
    occ_g, virt_width, aux_dev = factors.shape
    row_count = occ_g * virt_width
    groups = lax.axis_size("grp")
    shards = lax.axis_size("sh")
    slice_rows = row_count // shards
    my_group = lax.axis_index("grp")
    wide_mask = jnp.repeat(jnp.repeat(screen, BLK, axis=1), BLK, axis=2)
    own_block = (factors * wide_mask.astype(jnp.bfloat16)).reshape(row_count, aux_dev)
    occ_own = lax.dynamic_slice_in_dim(occ_energy, my_group * occ_g, occ_g)
    all_rows = (virt_energy[None, :] - occ_own[:, None]).reshape(-1)
    row_energy = lax.dynamic_slice_in_dim(all_rows, lax.axis_index("sh") * slice_rows, slice_rows)

    def update(running, partner, other_group):
        occ_other = lax.dynamic_slice_in_dim(occ_energy, other_group * occ_g, occ_g)
        col_energy = (virt_energy[None, :] - occ_other[:, None]).reshape(-1)
        coulomb = lax.psum_scatter(
            lax.dot_general(
                own_block, partner, (((1,), (1,)), ((), ())), preferred_element_type=jnp.float32
            ),
            "sh",
            scatter_dimension=0,
            tiled=True,
        )
        amplitude = (coulomb / (row_energy[:, None] + col_energy[None, :])).astype(jnp.bfloat16)
        full_amp = lax.all_gather(amplitude, "sh", axis=0, tiled=True)
        four_index = full_amp.reshape(occ_g, virt_width, occ_g, virt_width).astype(jnp.float32)
        combined = (2.0 * four_index - jnp.transpose(four_index, (0, 3, 2, 1))).astype(jnp.bfloat16)
        combined = combined.reshape(row_count, row_count)
        return running + jnp.dot(combined, partner, preferred_element_type=jnp.float32)

    gamma_sum = update(jnp.zeros((row_count, aux_dev), jnp.float32), own_block, my_group)

    def one_turn(turn_index, state_tuple):
        running, partner = state_tuple
        partner = passed_along(partner, "grp", 1)
        return (update(running, partner, (my_group - turn_index) % groups), partner)

    gamma_sum, moved = lax.fori_loop(1, groups, one_turn, (gamma_sum, own_block))
    gamma_local = gamma_sum.astype(jnp.bfloat16).reshape(occ_g, virt_width, aux_dev)
    return lax.all_to_all(gamma_local, "sh", split_axis=1, concat_axis=2, tiled=True)


def solution(mesh):
    placed = (P("grp", None, "sh"), P("grp", None, "sh"), P(), P())
    return jax.shard_map(
        on_device, mesh=mesh, in_specs=placed, out_specs=P("grp", "sh", None), check_vma=False
    )
```

profile of v0, /device:TPU:32, one launch (start us, length us, event | category | flops | bytes accessed | tf_op | source)
XLA Modules:
  0.0 2016.6 jit_solution(13149707756781648641)
XLA Ops:
  10.7 70.3 %reduce-scatter.11.cloned.1.call-done = f32[24,384]{1,0:T(8,128)} async-done(((f32[384,384]{1,0:T(8,128)}), f32[24,384]{1,0:T(8,128)}) %reduce-scatter.11.cloned.1.call-update) | async-done | bytes 36880
  114.9 1868.6 %while.17 = (s32[]{:T(128)}, f32[384,896]{1,0:T(8,128)S(1)}, bf16[384,896]{1,0:T(8,128)(2,1)S(1)}, bf16[384,896]{1,0:T(8,128)(2,1)S(1)}, f32[24]{0:T(128)S(1)}, ...) while((s32[]{:T(128)}, f32[384,896]{1,0:T(8,128)S(1)}, ...), condition=%wide.region_3.4_spmd, body=%wide.region_1.3_spmd.sunk | while | flops 529296768 | bytes 18964512 | solution.py:53
  131.5 68.3 %reduce-scatter.13.cloned.1.call-done = f32[24,384]{1,0:T(8,128)} async-done(((f32[384,384]{1,0:T(8,128)}), f32[24,384]{1,0:T(8,128)}) %reduce-scatter.13.cloned.1.call-update) | async-done | bytes 36880 | tf_op jit(solution)/shard_map/while
  255.8 68.7 %reduce-scatter.13.cloned.1.call-done = f32[24,384]{1,0:T(8,128)} async-done(((f32[384,384]{1,0:T(8,128)}), f32[24,384]{1,0:T(8,128)}) %reduce-scatter.13.cloned.1.call-update) | async-done | bytes 36880 | tf_op jit(solution)/shard_map/while
  325.4 34.0 %all_gather.15 = bf16[384,384]{1,0:T(8,128)(2,1)} all-gather(bf16[24,384]{1,0:T(8,128)(2,1)S(1)} %divide_convert_fusion.3), channel_id=1, replica_groups=mesh['grp'=16,'sh'=16] {'sh'}, dimensions={0}, use_global_device_ids=true | all-gather | bytes 313344 | tf_op jit(solution)/shard_map/while/body/eval_jaxpr/all_gather | solution.py:40
  380.7 68.4 %reduce-scatter.13.cloned.1.call-done = f32[24,384]{1,0:T(8,128)} async-done(((f32[384,384]{1,0:T(8,128)}), f32[24,384]{1,0:T(8,128)}) %reduce-scatter.13.cloned.1.call-update) | async-done | bytes 36880 | tf_op jit(solution)/shard_map/while
  505.1 68.5 %reduce-scatter.13.cloned.1.call-done = f32[24,384]{1,0:T(8,128)} async-done(((f32[384,384]{1,0:T(8,128)}), f32[24,384]{1,0:T(8,128)}) %reduce-scatter.13.cloned.1.call-update) | async-done | bytes 36880 | tf_op jit(solution)/shard_map/while
  574.5 34.0 %all_gather.15 = bf16[384,384]{1,0:T(8,128)(2,1)} all-gather(bf16[24,384]{1,0:T(8,128)(2,1)S(1)} %divide_convert_fusion.3), channel_id=1, replica_groups=mesh['grp'=16,'sh'=16] {'sh'}, dimensions={0}, use_global_device_ids=true | all-gather | bytes 313344 | tf_op jit(solution)/shard_map/while/body/eval_jaxpr/all_gather | solution.py:40
  629.8 68.3 %reduce-scatter.13.cloned.1.call-done = f32[24,384]{1,0:T(8,128)} async-done(((f32[384,384]{1,0:T(8,128)}), f32[24,384]{1,0:T(8,128)}) %reduce-scatter.13.cloned.1.call-update) | async-done | bytes 36880 | tf_op jit(solution)/shard_map/while
  754.2 68.5 %reduce-scatter.13.cloned.1.call-done = f32[24,384]{1,0:T(8,128)} async-done(((f32[384,384]{1,0:T(8,128)}), f32[24,384]{1,0:T(8,128)}) %reduce-scatter.13.cloned.1.call-update) | async-done | bytes 36880 | tf_op jit(solution)/shard_map/while
  823.6 34.0 %all_gather.15 = bf16[384,384]{1,0:T(8,128)(2,1)} all-gather(bf16[24,384]{1,0:T(8,128)(2,1)S(1)} %divide_convert_fusion.3), channel_id=1, replica_groups=mesh['grp'=16,'sh'=16] {'sh'}, dimensions={0}, use_global_device_ids=true | all-gather | bytes 313344 | tf_op jit(solution)/shard_map/while/body/eval_jaxpr/all_gather | solution.py:40
  878.9 68.3 %reduce-scatter.13.cloned.1.call-done = f32[24,384]{1,0:T(8,128)} async-done(((f32[384,384]{1,0:T(8,128)}), f32[24,384]{1,0:T(8,128)}) %reduce-scatter.13.cloned.1.call-update) | async-done | bytes 36880 | tf_op jit(solution)/shard_map/while
  948.0 34.1 %all_gather.15 = bf16[384,384]{1,0:T(8,128)(2,1)} all-gather(bf16[24,384]{1,0:T(8,128)(2,1)S(1)} %divide_convert_fusion.3), channel_id=1, replica_groups=mesh['grp'=16,'sh'=16] {'sh'}, dimensions={0}, use_global_device_ids=true | all-gather | bytes 313344 | tf_op jit(solution)/shard_map/while/body/eval_jaxpr/all_gather | solution.py:40
  1003.5 68.3 %reduce-scatter.13.cloned.1.call-done = f32[24,384]{1,0:T(8,128)} async-done(((f32[384,384]{1,0:T(8,128)}), f32[24,384]{1,0:T(8,128)}) %reduce-scatter.13.cloned.1.call-update) | async-done | bytes 36880 | tf_op jit(solution)/shard_map/while
  1127.8 68.5 %reduce-scatter.13.cloned.1.call-done = f32[24,384]{1,0:T(8,128)} async-done(((f32[384,384]{1,0:T(8,128)}), f32[24,384]{1,0:T(8,128)}) %reduce-scatter.13.cloned.1.call-update) | async-done | bytes 36880 | tf_op jit(solution)/shard_map/while
  1252.4 68.4 %reduce-scatter.13.cloned.1.call-done = f32[24,384]{1,0:T(8,128)} async-done(((f32[384,384]{1,0:T(8,128)}), f32[24,384]{1,0:T(8,128)}) %reduce-scatter.13.cloned.1.call-update) | async-done | bytes 36880 | tf_op jit(solution)/shard_map/while
  1321.6 34.0 %all_gather.15 = bf16[384,384]{1,0:T(8,128)(2,1)} all-gather(bf16[24,384]{1,0:T(8,128)(2,1)S(1)} %divide_convert_fusion.3), channel_id=1, replica_groups=mesh['grp'=16,'sh'=16] {'sh'}, dimensions={0}, use_global_device_ids=true | all-gather | bytes 313344 | tf_op jit(solution)/shard_map/while/body/eval_jaxpr/all_gather | solution.py:40
  1376.9 68.5 %reduce-scatter.13.cloned.1.call-done = f32[24,384]{1,0:T(8,128)} async-done(((f32[384,384]{1,0:T(8,128)}), f32[24,384]{1,0:T(8,128)}) %reduce-scatter.13.cloned.1.call-update) | async-done | bytes 36880 | tf_op jit(solution)/shard_map/while
  1446.2 34.0 %all_gather.15 = bf16[384,384]{1,0:T(8,128)(2,1)} all-gather(bf16[24,384]{1,0:T(8,128)(2,1)S(1)} %divide_convert_fusion.3), channel_id=1, replica_groups=mesh['grp'=16,'sh'=16] {'sh'}, dimensions={0}, use_global_device_ids=true | all-gather | bytes 313344 | tf_op jit(solution)/shard_map/while/body/eval_jaxpr/all_gather | solution.py:40
  1501.5 68.5 %reduce-scatter.13.cloned.1.call-done = f32[24,384]{1,0:T(8,128)} async-done(((f32[384,384]{1,0:T(8,128)}), f32[24,384]{1,0:T(8,128)}) %reduce-scatter.13.cloned.1.call-update) | async-done | bytes 36880 | tf_op jit(solution)/shard_map/while
  1625.9 68.6 %reduce-scatter.13.cloned.1.call-done = f32[24,384]{1,0:T(8,128)} async-done(((f32[384,384]{1,0:T(8,128)}), f32[24,384]{1,0:T(8,128)}) %reduce-scatter.13.cloned.1.call-update) | async-done | bytes 36880 | tf_op jit(solution)/shard_map/while
  1750.3 68.6 %reduce-scatter.13.cloned.1.call-done = f32[24,384]{1,0:T(8,128)} async-done(((f32[384,384]{1,0:T(8,128)}), f32[24,384]{1,0:T(8,128)}) %reduce-scatter.13.cloned.1.call-update) | async-done | bytes 36880 | tf_op jit(solution)/shard_map/while
  1875.1 68.5 %reduce-scatter.13.cloned.1.call-done = f32[24,384]{1,0:T(8,128)} async-done(((f32[384,384]{1,0:T(8,128)}), f32[24,384]{1,0:T(8,128)}) %reduce-scatter.13.cloned.1.call-update) | async-done | bytes 36880 | tf_op jit(solution)/shard_map/while
  1944.4 34.3 %all_gather.15 = bf16[384,384]{1,0:T(8,128)(2,1)} all-gather(bf16[24,384]{1,0:T(8,128)(2,1)S(1)} %divide_convert_fusion.3), channel_id=1, replica_groups=mesh['grp'=16,'sh'=16] {'sh'}, dimensions={0}, use_global_device_ids=true | all-gather | bytes 313344 | tf_op jit(solution)/shard_map/while/body/eval_jaxpr/all_gather | solution.py:40
  (275 shorter events, 666.6 us)
Async XLA Ops:
  6.5 74.5 %reduce-scatter.11.cloned.1.call-start = ((), (), s32[]{:S(2)}) async-start(), calls=%async_computation.3 | async-start | bytes 626688
  115.0 84.8 %reduce-scatter.13.cloned.1.call-start = ((), (), s32[]{:S(2)}) async-start(), calls=%async_computation.4 | async-start | bytes 626688 | tf_op jit(solution)/shard_map/while
  115.0 14.1 collective-permute-start
  239.4 85.1 %reduce-scatter.13.cloned.1.call-start = ((), (), s32[]{:S(2)}) async-start(), calls=%async_computation.4 | async-start | bytes 626688 | tf_op jit(solution)/shard_map/while
  239.4 14.0 collective-permute-start
  364.3 84.8 %reduce-scatter.13.cloned.1.call-start = ((), (), s32[]{:S(2)}) async-start(), calls=%async_computation.4 | async-start | bytes 626688 | tf_op jit(solution)/shard_map/while
  364.3 14.0 collective-permute-start
  488.7 84.9 %reduce-scatter.13.cloned.1.call-start = ((), (), s32[]{:S(2)}) async-start(), calls=%async_computation.4 | async-start | bytes 626688 | tf_op jit(solution)/shard_map/while
  488.7 14.0 collective-permute-start
  613.4 84.7 %reduce-scatter.13.cloned.1.call-start = ((), (), s32[]{:S(2)}) async-start(), calls=%async_computation.4 | async-start | bytes 626688 | tf_op jit(solution)/shard_map/while
  737.8 84.9 %reduce-scatter.13.cloned.1.call-start = ((), (), s32[]{:S(2)}) async-start(), calls=%async_computation.4 | async-start | bytes 626688 | tf_op jit(solution)/shard_map/while
  862.5 84.7 %reduce-scatter.13.cloned.1.call-start = ((), (), s32[]{:S(2)}) async-start(), calls=%async_computation.4 | async-start | bytes 626688 | tf_op jit(solution)/shard_map/while
  862.5 14.0 collective-permute-start
  987.1 84.7 %reduce-scatter.13.cloned.1.call-start = ((), (), s32[]{:S(2)}) async-start(), calls=%async_computation.4 | async-start | bytes 626688 | tf_op jit(solution)/shard_map/while
  987.1 14.0 collective-permute-start
  1111.4 84.9 %reduce-scatter.13.cloned.1.call-start = ((), (), s32[]{:S(2)}) async-start(), calls=%async_computation.4 | async-start | bytes 626688 | tf_op jit(solution)/shard_map/while
  1236.0 84.8 %reduce-scatter.13.cloned.1.call-start = ((), (), s32[]{:S(2)}) async-start(), calls=%async_computation.4 | async-start | bytes 626688 | tf_op jit(solution)/shard_map/while
  1236.0 14.0 collective-permute-start
  1360.5 84.9 %reduce-scatter.13.cloned.1.call-start = ((), (), s32[]{:S(2)}) async-start(), calls=%async_computation.4 | async-start | bytes 626688 | tf_op jit(solution)/shard_map/while
  1485.1 84.9 %reduce-scatter.13.cloned.1.call-start = ((), (), s32[]{:S(2)}) async-start(), calls=%async_computation.4 | async-start | bytes 626688 | tf_op jit(solution)/shard_map/while
  1609.5 85.0 %reduce-scatter.13.cloned.1.call-start = ((), (), s32[]{:S(2)}) async-start(), calls=%async_computation.4 | async-start | bytes 626688 | tf_op jit(solution)/shard_map/while
  1733.9 85.0 %reduce-scatter.13.cloned.1.call-start = ((), (), s32[]{:S(2)}) async-start(), calls=%async_computation.4 | async-start | bytes 626688 | tf_op jit(solution)/shard_map/while
  1858.7 84.9 %reduce-scatter.13.cloned.1.call-start = ((), (), s32[]{:S(2)}) async-start(), calls=%async_computation.4 | async-start | bytes 626688 | tf_op jit(solution)/shard_map/while
  1858.7 14.0 collective-permute-start
  (24 other events, 115.7 us)
Sparse Core Ops, SparseCore 0:
  10.0 71.0 reduce-scatter.10
  130.6 69.1 reduce-scatter.12
  254.9 69.5 reduce-scatter.12
  379.8 69.2 reduce-scatter.12
  504.2 69.3 reduce-scatter.12
  628.9 69.1 reduce-scatter.12
  753.3 69.3 reduce-scatter.12
  878.0 69.1 reduce-scatter.12
  1002.5 69.1 reduce-scatter.12
  1126.9 69.3 reduce-scatter.12
  1251.5 69.2 reduce-scatter.12
  1376.0 69.3 reduce-scatter.12
  1500.6 69.3 reduce-scatter.12
  1625.0 69.4 reduce-scatter.12
  1749.4 69.4 reduce-scatter.12
  1874.2 69.3 reduce-scatter.12
where the time goes:
time: 2020 us
  waiting for transfers between devices  1310 us (65%)
  blocking collectives  566 us (28%)
  local copies, waits for them, and re-layouts  63.4 us (3%)
  other arithmetic  33.9 us (2%)
  matrix products  31.6 us (2%)
    while x30, waiting for transfers between devices  1030 us
    all_gather x16, blocking collectives, update(): full_amp = lax.all_gather(amplitude, 'sh', axis=0, tiled=True)  541 us
    ppermute x15, waiting for transfers between devices, passed_along(): return lax.ppermute(value, axis, pairs)  210 us
    unnamed x2, waiting for transfers between devices  70.3 us
  transfers between devices with their start and end apart: 31, of which 31 were waited for; matrix products, arithmetic and copies ran while one was open for 1% of the time, Pallas kernels for 0%

commit v1 on v0

v1 whole, which is shorter than its diff:
```python
import functools

import jax
import jax.numpy as jnp
from jax import lax
from jax.experimental import pallas as pl
from jax.experimental.pallas import tpu as pltpu
from jax.sharding import Mesh, PartitionSpec as P

BLK = 128
NY, NXH, NC, NZ, NXL = 4, 2, 2, 8, 2
GRP = ("y", "xh", "core")
SH = ("z", "xl")
X = ("xh", "xl")
BF = jnp.bfloat16
F32 = jnp.float32


def flip_x(value, bits):
    return lax.ppermute(value, X, [(i, i ^ bits) for i in range(NXH * NXL)])


def shift(value, axis, steps):
    count = lax.axis_size(axis)
    return lax.ppermute(value, axis, [(i, (i + steps) % count) for i in range(count)])


def flip_core(value):
    return lax.ppermute(value, "core", [(0, 1), (1, 0)])


def coulomb_kernel(same_ref, own, xlf, bof, xh0, xh1, *refs):
    out = refs[-1]
    near, far = refs[0:5], refs[5:10]
    hr = xh0.shape[0]

    def dot(a, b):
        return lax.dot_general(a[...], b[...], (((1,), (1,)), ((), ())), preferred_element_type=F32)

    def run(mine, other):
        def put(block, rows, left, right):
            columns = [(0, slice(0, 2 * hr), 0), (1, slice(0, 2 * hr), 1), (2, slice(0, hr), 2),
                       (2, slice(hr, 2 * hr), 3), (3, slice(0, 2 * hr), 4)]
            for d, cols, piece in columns:
                out[block + d, rows, cols] = dot(left, mine[piece]) + dot(right, other[piece])

        put(0, slice(0, 2 * hr), own, xlf)
        put(4, slice(0, hr), xh0, bof.at[pl.ds(0, hr)])
        put(4, slice(hr, 2 * hr), xh1, bof.at[pl.ds(hr, hr)])

    @pl.when(same_ref[0] == 1)
    def _():
        run(near, far)

    @pl.when(same_ref[0] == 0)
    def _():
        run(far, near)


def gamma_kernel(pos_ref, comb, *refs, base, wide):
    near, far, outs = refs[0:5], refs[5:10], refs[10:]
    half = near[0].shape[1]
    hr = near[2].shape[0]
    z, xl = pos_ref[0], pos_ref[1]
    for fl in range(2):
        h = lax.rem(xl + fl, 2)
        lhs = [comb[base + d, h] for d in range(NY)]
        parts = [lhs[0], lhs[1], lhs[2][:, :hr], lhs[2][:, hr:], lhs[3]]
        for k, pieces in enumerate((near, far)):
            acc = jnp.dot(parts[0], pieces[0][...], preferred_element_type=F32)
            for p in range(1, 5):
                acc += jnp.dot(parts[p], pieces[p][...], preferred_element_type=F32)
            rows = acc.shape[0] // NZ
            for zp in range(NZ):
                outs[fl][lax.rem(zp + NZ - z, NZ), :, k * half:(k + 1) * half] = acc[zp * rows:(zp + 1) * rows].astype(
                    outs[fl].dtype
                )


def assemble_kernel(pos_ref, *refs):
    out = refs[-1]
    z, core = pos_ref[0], pos_ref[2]
    half = refs[0].shape[1] // 2
    for k in range(NZ):
        source = lax.rem(z + NZ - k, NZ)
        for part in range(2):
            start = pl.multiple_of(source * 2 * half + lax.rem(core + part, 2) * half, 128)
            out[:, pl.ds(start, half)] = refs[k][:, part * half:(part + 1) * half]


def on_device(factors, screen, occ_energy, virt_energy):
    occ_g, virt, aux = factors.shape
    rows = occ_g * virt
    hr = rows // 2
    y, xh, c, z, xl = (lax.axis_index(n) for n in ("y", "xh", "core", "z", "xl"))
    wide_mask = jnp.repeat(jnp.repeat(screen, BLK, axis=1), BLK, axis=2)
    own = (factors * wide_mask.astype(BF)).reshape(rows, aux)

    with jax.named_scope("gather"):
        j0 = lax.ppermute(own, ("core", "xl"), [(0, 0), (1, 2), (2, 1), (3, 3)])
        xlf = flip_x(own, 1)
        bof = flip_x(own, 3)
        j1 = shift(j0, "y", 1)
        j3 = shift(j0, "y", -1)
        xh0 = flip_x(xlf[:hr], 3)
        xh1 = flip_x(bof[hr:], 1)
        j2a = shift(j1[:hr], "y", 1)
        j2b = shift(j3[hr:], "y", -1)
        near = [j0, j1, j2a, j2b, j3]
        far = [flip_core(p) for p in near]

    vmem = pl.BlockSpec(memory_space=pltpu.VMEM)
    smem = pl.BlockSpec(memory_space=pltpu.SMEM)
    with jax.named_scope("coulomb"):
        same = (xl == c).astype(jnp.int32).reshape(1)
        partial = pl.pallas_call(
            coulomb_kernel,
            out_shape=jax.ShapeDtypeStruct((NZ, rows, rows), F32),
            in_specs=[smem] + [vmem] * 15,
            out_specs=vmem,
            compiler_params=pltpu.CompilerParams(vmem_limit_bytes=48 << 20),
        )(same, own, xlf, bof, xh0, xh1, *near, *far)
        block = lax.psum_scatter(partial.reshape(NZ * rows, rows), "z", scatter_dimension=0, tiled=True)

    with jax.named_scope("combined"):
        e, d = z // NY, z % NY
        row_group = (y * NXH + (xh + e) % NXH) * NC + c
        col_group = (((y + NY - d) % NY) * NXH + xh) * NC + xl
        row_occ = lax.dynamic_slice_in_dim(occ_energy, row_group * occ_g, occ_g)
        col_occ = lax.dynamic_slice_in_dim(occ_energy, col_group * occ_g, occ_g)
        row_energy = (virt_energy[None, :] - row_occ[:, None]).reshape(-1)
        col_energy = (virt_energy[None, :] - col_occ[:, None]).reshape(-1)
        amplitude = (block / (row_energy[:, None] + col_energy[None, :])).astype(BF)
        four = amplitude.reshape(occ_g, virt, occ_g, virt).astype(F32)
        comb = (2.0 * four - jnp.transpose(four, (0, 3, 2, 1))).astype(BF)
        comb = comb.reshape(occ_g, NZ, NXL, virt // (NZ * NXL), rows)
        comb = jnp.transpose(comb, (2, 1, 0, 3, 4)).reshape(NXL, hr, rows)
        comb = lax.all_gather(comb, "z")

    with jax.named_scope("gamma"):
        pos = jnp.stack([z, xl, c]).astype(jnp.int32)
        piece = hr // NZ

        def gamma_of(base, types):
            return pl.pallas_call(
                functools.partial(gamma_kernel, base=base, wide=2 * aux),
                out_shape=[jax.ShapeDtypeStruct((NZ, piece, 2 * aux), t) for t in types],
                in_specs=[smem] + [vmem] * 11,
                out_specs=[vmem] * 2,
                compiler_params=pltpu.CompilerParams(vmem_limit_bytes=48 << 20),
            )(pos, comb, *near, *far)

        to_xh, to_both = gamma_of(NY, (BF, BF))
        from_both = flip_x(to_both, 3)
        from_xh = flip_x(to_xh, 2)
        mine, to_xl = gamma_of(0, (F32, BF))
        from_xl = flip_x(to_xl, 1)
        total = (mine + from_xl.astype(F32) + from_both.astype(F32) + from_xh.astype(F32)).astype(BF)

    with jax.named_scope("spread"):
        got = [total[0]] + [shift(total[k], "z", k) for k in range(1, NZ)]
        out = pl.pallas_call(
            assemble_kernel,
            out_shape=jax.ShapeDtypeStruct((piece, NZ * 2 * aux), BF),
            in_specs=[smem] + [vmem] * NZ,
            out_specs=vmem,
            compiler_params=pltpu.CompilerParams(vmem_limit_bytes=16 << 20),
        )(pos, *got)
    return out.reshape(occ_g, piece // occ_g, NZ * 2 * aux)


def solution(mesh):
    split = Mesh(mesh.devices.reshape(NY, NXH, NC, NZ, NXL), ("y", "xh", "core", "z", "xl"))
    placed = (P(GRP, None, SH), P(GRP, None, SH), P(), P())
    return jax.shard_map(on_device, mesh=split, in_specs=placed, out_specs=P(GRP, SH, None), check_vma=False)
```

time: 2020 us -> 250 us (0.12)
  waiting for transfers between devices: 1310 us -> 158 us
  blocking collectives: 566 us -> 0 us
  local copies, waits for them, and re-layouts: 63.4 us -> 13.3 us
  starting transfers between devices: 0.19 us -> 34.5 us
  matrix products: 31.6 us -> 0 us
  other arithmetic: 33.9 us -> 4.95 us
  Pallas kernels: 0 us -> 24.6 us
    while x30 -> x0, waiting for transfers between devices: 1030 us -> none
    all_gather x16 -> x0, blocking collectives: 541 us -> none  [update(): full_amp = lax.all_gather(amplitude, 'sh', axis=0, tiled=True)]
    ppermute x15 -> x24, waiting for transfers between devices: 210 us -> 57.5 us  [the longest x7 42.8 us: flip_x(): return lax.ppermute(value, X, [(i, i ^ bits) for i in range(NXH * NXL)])]
    unnamed x2, waiting for transfers between devices: 70.3 us -> 0.03 us
    reduce_scatter x0 -> x1, waiting for transfers between devices: none -> 58.9 us  [on_device(): lax.psum_scatter(partial.reshape(NZ * rows, rows), 'z', scatter_dimension...]
    all_gather x0 -> x1, waiting for transfers between devices: none -> 41.6 us  [on_device(): comb = lax.all_gather(comb, 'z')]
    convert_element_type x48 -> x3, local copies, waits for them, and re-layouts: 40 us -> 1.48 us  [the longest x1 1 us: on_device(): comb = (2.0 * four - jnp.transpose(four, (0, 3, 2, 1))).astype(BF)]
    ppermute x15 -> x24, starting transfers between devices: 0.12 us -> 34.2 us  [the longest x11 20.8 us: shift(): lax.ppermute(value, axis, [(i, (i + steps) % count) for i in range(count)])]
  transfers between devices with their start and end apart: 31 -> 26, of which waited for: 31 -> 15; matrix products, arithmetic and copies ran while one was open for 1% -> 0% of each run, Pallas kernels for 0% -> 3%
where the time goes in v1:
time: 250 us; the launch traced here: 249 us
  waiting for transfers between devices  158 us (63%)
  starting transfers between devices  34.5 us (14%)
  Pallas kernels  24.6 us (10%)
  between operations  13.7 us (5%)
  local copies, waits for them, and re-layouts  13.3 us (5%)
  other arithmetic  4.95 us (2%)
    reduce_scatter x1, waiting for transfers between devices, on_device(): lax.psum_scatter(partial.reshape(NZ * rows, rows), 'z', scatter_dimension...  58.9 us
    ppermute x7, waiting for transfers between devices, flip_x(): return lax.ppermute(value, X, [(i, i ^ bits) for i in range(NXH * NXL)])  42.8 us
    all_gather x1, waiting for transfers between devices, on_device(): comb = lax.all_gather(comb, 'z')  41.6 us
    ppermute x11, starting transfers between devices, shift(): lax.ppermute(value, axis, [(i, (i + steps) % count) for i in range(count)])  20.8 us
    ppermute x11, waiting for transfers between devices, shift(): lax.ppermute(value, axis, [(i, (i + steps) % count) for i in range(count)])  12.7 us
    pallas_call x2, Pallas kernels, gamma_of(): pl.pallas_call(functools.partial(gamma_kernel, base=base, wide=2 * aux),...  12 us
    ppermute x7, starting transfers between devices, flip_x(): return lax.ppermute(value, X, [(i, i ^ bits) for i in range(NXH * NXL)])  11.8 us
    pallas_call x1, Pallas kernels, on_device(): pl.pallas_call(coulomb_kernel, out_shape=jax.ShapeDtypeStruct((NZ, rows,...  11.1 us
  transfers between devices with their start and end apart: 26, of which 15 were waited for; matrix products, arithmetic and copies ran while one was open for 0% of the time, Pallas kernels for 3%

profile of v1, /device:TPU:32, one launch (start us, length us, event | category | flops | bytes accessed | tf_op | source)
XLA Modules:
  0.0 249.0 jit_solution(2454286687931154074)
XLA Ops:
  9.2 2.8 %collective-permute-start = (bf16[384,896]{1,0:T(8,128)(2,1)S(1)}, bf16[384,896]{1,0:T(8,128)(2,1)S(1)}, u32[]{:S(2)}, u32[]{:S(2)}) collective-permute-start(bf16[384,896]{1,0:T(8,128)(2,1)S(1)} %bitcast.42), channel_id=1, source_target_pairs={{0,1},{1,0},{32,33},{33,32},{2,3},{3,2},{34,35},{35,34},{4,5},{5,4... | collective-permute-start | bytes 2064392 | tf_op jit(solution)/shard_map/gather/ppermute | solution.py:20
  16.9 18.7 %collective-permute-done.xlf = bf16[384,896]{1,0:T(8,128)(2,1)S(1)} collective-permute-done((bf16[384,896]{1,0:T(8,128)(2,1)S(1)}, bf16[384,896]{1,0:T(8,128)(2,1)S(1)}, u32[]{:S(2)}, u32[]{:S(2)}) %collective-permute-start) | collective-permute-done | bytes 688160 | tf_op jit(solution)/shard_map/gather/ppermute | solution.py:20
  36.8 2.0 collective-permute-start.3
  40.5 1.7 collective-permute-start.8
  42.2 4.5 %collective-permute-done.2.xh0 = bf16[192,896]{1,0:T(8,128)(2,1)S(1)} collective-permute-done((bf16[192,896]{1,0:T(8,128)(2,1)S(1)}, bf16[192,896]{1,0:T(8,128)(2,1)S(1)}, u32[]{:S(2)}, u32[]{:S(2)}) %collective-permute-start.2) | collective-permute-done | bytes 344096 | tf_op jit(solution)/shard_map/gather/ppermute | solution.py:20
  48.7 2.0 collective-permute-done.6.refs_2_
  59.3 11.1 %coulomb.1 = f32[8,384,384]{2,1,0:T(8,128)} custom-call(s32[1]{0:T(128)} %bitcast.3.same_ref, bf16[384,896]{1,0:T(8,128)(2,1)S(1)} %bitcast.44, bf16[384,896]{1,0:T(8,128)(2,1)S(1)} %copy-done.7, bf16[384,896]{1,0:T(8,128)(2,1)S(1)} %copy-done.9, bf16[192,896]{1,0:T(8,128)(2,1)S(1)} %copy-done.11, bf16[192,896]{1,0:T(8,128)(2,1)S(1)} %copy-done.13, ...), custom_call_target="tpu_custom_call" | custom-call | tf_op jit(solution)/shard_map/coulomb/pallas_call | solution.py:116
  71.2 58.9 %reduce-scatter.2.cloned.1.call-done = f32[384,384]{1,0:T(8,128)} async-done(((f32[3072,384]{1,0:T(8,128)}), f32[384,384]{1,0:T(8,128)}) %reduce-scatter.2.cloned.1.call-update) | async-done | bytes 589840 | tf_op jit(solution)/shard_map/coulomb/reduce_scatter | solution.py:123
  132.9 2.0 reshape.66
  134.8 1.7 copy.17
  136.7 41.6 %all-gather.2.cloned.1.call-done.comb = bf16[8,2,192,384]{3,2,1,0:T(8,128)(2,1)} async-done(((bf16[1,2,192,384]{3,2,1,0:T(8,128)(2,1)}), bf16[8,2,192,384]{3,2,1,0:T(8,128)(2,1)}) %all-gather.2.cloned.1.call-update) | async-done | bytes 2359312 | tf_op jit(solution)/shard_map/combined/all_gather | solution.py:138
  178.3 5.6 %gamma.3 = (bf16[8,24,1792]{2,1,0:T(8,128)(2,1)S(1)}, bf16[8,24,1792]{2,1,0:T(8,128)(2,1)S(1)}) custom-call(s32[3]{0:T(128)S(1)} %pad_add_fusion.pos_ref, bf16[8,2,192,384]{3,2,1,0:T(8,128)(2,1)} %all-gather.2.cloned.1.call-done.comb, bf16[384,896]{1,0:T(8,128)(2,1)S(1)} %collective-permute-done.4.refs_0_, ...), custom_call_target="tpu_custom_call" | custom-call | tf_op jit(solution)/shard_map/gamma/pallas_call | solution.py:145
  183.9 3.1 %collective-permute-start.16 = (bf16[8,24,1792]{2,1,0:T(8,128)(2,1)S(1)}, bf16[8,24,1792]{2,1,0:T(8,128)(2,1)S(1)}, u32[]{:S(2)}, u32[]{:S(2)}) collective-permute-start(bf16[8,24,1792]{2,1,0:T(8,128)(2,1)S(1)} %get-tuple-element.12), channel_id=1, source_target_pairs={{0,32},{1,33},{32,0},{33,1},{2,34},{3,35},{34,2},{35,3},{4,36},{5,... | collective-permute-start | bytes 2064392 | tf_op jit(solution)/shard_map/gamma/ppermute | solution.py:20
  188.1 6.5 %gamma.2 = (f32[8,24,1792]{2,1,0:T(8,128)}, bf16[8,24,1792]{2,1,0:T(8,128)(2,1)S(1)}) custom-call(s32[3]{0:T(128)S(1)} %pad_add_fusion.pos_ref, bf16[8,2,192,384]{3,2,1,0:T(8,128)(2,1)} %all-gather.2.cloned.1.call-done.comb, bf16[384,896]{1,0:T(8,128)(2,1)S(1)} %collective-permute-done.4.refs_0_, bf16[384,896]{1,0:T(8,128)(2,1)S(1)} %collective-permute-done.5.refs_1_, ...), custom_call_target="tpu_custom_call" | custom-call | tf_op jit(solution)/shard_map/gamma/pallas_call | solution.py:145
  194.6 9.3 %collective-permute-done.16 = bf16[8,24,1792]{2,1,0:T(8,128)(2,1)S(1)} collective-permute-done((bf16[8,24,1792]{2,1,0:T(8,128)(2,1)S(1)}, bf16[8,24,1792]{2,1,0:T(8,128)(2,1)S(1)}, u32[]{:S(2)}, u32[]{:S(2)}) %collective-permute-start.16) | collective-permute-done | bytes 688160 | tf_op jit(solution)/shard_map/gamma/ppermute | solution.py:20
  203.8 10.3 %collective-permute-done.15 = bf16[8,24,1792]{2,1,0:T(8,128)(2,1)S(1)} collective-permute-done((bf16[8,24,1792]{2,1,0:T(8,128)(2,1)S(1)}, bf16[8,24,1792]{2,1,0:T(8,128)(2,1)S(1)}, u32[]{:S(2)}, u32[]{:S(2)}) %collective-permute-start.15) | collective-permute-done | bytes 688160 | tf_op jit(solution)/shard_map/gamma/ppermute | solution.py:20
  217.1 2.0 collective-permute-start.18
  219.1 2.3 collective-permute-start.19
  221.4 3.0 %collective-permute-start.20 = (bf16[24,1792]{1,0:T(8,128)(2,1)S(1)}, bf16[24,1792]{1,0:T(8,128)(2,1)S(1)}, u32[]{:S(2)}, u32[]{:S(2)}) collective-permute-start(bf16[24,1792]{1,0:T(8,128)(2,1)S(1)} %get-tuple-element.16), channel_id=1, source_target_pairs={{0,8},{2,10},{4,12},{6,14},{8,0},{10,2},{12,4},{14,6},{1,9},{3,11}... | collective-permute-start | bytes 258056 | tf_op jit(solution)/shard_map/spread/ppermute | solution.py:25
  224.4 2.8 %collective-permute-start.21 = (bf16[24,1792]{1,0:T(8,128)(2,1)S(1)}, bf16[24,1792]{1,0:T(8,128)(2,1)S(1)}, u32[]{:S(2)}, u32[]{:S(2)}) collective-permute-start(bf16[24,1792]{1,0:T(8,128)(2,1)S(1)} %get-tuple-element.15), channel_id=1, source_target_pairs={{0,10},{2,12},{4,14},{6,0},{8,2},{10,4},{12,6},{14,8},{1,11},{3,13... | collective-permute-start | bytes 258056 | tf_op jit(solution)/shard_map/spread/ppermute | solution.py:25
  228.3 1.7 collective-permute-start.23
  230.1 2.7 %collective-permute-done.19.refs_3_ = bf16[24,1792]{1,0:T(8,128)(2,1)S(1)} collective-permute-done((bf16[24,1792]{1,0:T(8,128)(2,1)S(1)}, bf16[24,1792]{1,0:T(8,128)(2,1)S(1)}, u32[]{:S(2)}, u32[]{:S(2)}) %collective-permute-start.19) | collective-permute-done | bytes 86048 | tf_op jit(solution)/shard_map/spread/ppermute | solution.py:25
  232.8 5.2 %collective-permute-done.21.refs_5_ = bf16[24,1792]{1,0:T(8,128)(2,1)S(1)} collective-permute-done((bf16[24,1792]{1,0:T(8,128)(2,1)S(1)}, bf16[24,1792]{1,0:T(8,128)(2,1)S(1)}, u32[]{:S(2)}, u32[]{:S(2)}) %collective-permute-start.21) | collective-permute-done | bytes 86048 | tf_op jit(solution)/shard_map/spread/ppermute | solution.py:25
  238.4 2.2 collective-permute-done.23.refs_7_
  (87 shorter events, 31.8 us)
Async XLA Ops:
  6.5 123.5 %reduce-scatter.2.cloned.1.call-start = ((), (), s32[]{:S(2)}) async-start(), calls=%async_computation.1 | async-start | bytes 5308416 | tf_op jit(solution)/shard_map/coulomb/reduce_scatter | solution.py:123
  8.5 5.1 %collective-permute-start.4 = (bf16[384,896]{1,0:T(8,128)(2,1)S(1)}, bf16[384,896]{1,0:T(8,128)(2,1)S(1)}, u32[]{:S(2)}, u32[]{:S(2)}) collective-permute-start(bf16[384,896]{1,0:T(8,128)(2,1)S(1)} %bitcast.41), channel_id=1, source_target_pairs={{0,0},{1,16},{16,1},{17,17},{2,2},{3,18},{18,3},{19,19},{4,4},{5,2... | collective-permute-start | bytes 2064392 | tf_op jit(solution)/shard_map/gather/ppermute | solution.py:100
  9.2 26.3 %collective-permute-start = (bf16[384,896]{1,0:T(8,128)(2,1)S(1)}, bf16[384,896]{1,0:T(8,128)(2,1)S(1)}, u32[]{:S(2)}, u32[]{:S(2)}) collective-permute-start(bf16[384,896]{1,0:T(8,128)(2,1)S(1)} %bitcast.42), channel_id=1, source_target_pairs={{0,1},{1,0},{32,33},{33,32},{2,3},{3,2},{34,35},{35,34},{4,5},{5,4... | collective-permute-start | bytes 2064392 | tf_op jit(solution)/shard_map/gather/ppermute | solution.py:20
  12.0 24.7 %collective-permute-start.1 = (bf16[384,896]{1,0:T(8,128)(2,1)S(1)}, bf16[384,896]{1,0:T(8,128)(2,1)S(1)}, u32[]{:S(2)}, u32[]{:S(2)}) collective-permute-start(bf16[384,896]{1,0:T(8,128)(2,1)S(1)} %bitcast.43), channel_id=1, source_target_pairs={{0,33},{1,32},{32,1},{33,0},{2,35},{3,34},{34,3},{35,2},{4,37},{5,... | collective-permute-start | bytes 2064392 | tf_op jit(solution)/shard_map/gather/ppermute | solution.py:20
  13.6 25.1 %collective-permute-start.5 = (bf16[384,896]{1,0:T(8,128)(2,1)S(1)}, bf16[384,896]{1,0:T(8,128)(2,1)S(1)}, u32[]{:S(2)}, u32[]{:S(2)}) collective-permute-start(bf16[384,896]{1,0:T(8,128)(2,1)S(1)} %collective-permute-done.4.refs_0_), channel_id=1, source_target_pairs={{0,64},{64,128},{128,192},{192,0},{1,65},{65,129},{129,193},{193,1... | collective-permute-start | bytes 2064392 | tf_op jit(solution)/shard_map/gather/ppermute | solution.py:25
  15.2 25.2 %collective-permute-start.7 = (bf16[384,896]{1,0:T(8,128)(2,1)S(1)}, bf16[384,896]{1,0:T(8,128)(2,1)S(1)}, u32[]{:S(2)}, u32[]{:S(2)}) collective-permute-start(bf16[384,896]{1,0:T(8,128)(2,1)S(1)} %collective-permute-done.4.refs_0_), channel_id=1, source_target_pairs={{0,192},{64,0},{128,64},{192,128},{1,193},{65,1},{129,65},{193,129... | collective-permute-start | bytes 2064392 | tf_op jit(solution)/shard_map/gather/ppermute | solution.py:25
  35.6 11.1 %collective-permute-start.2 = (bf16[192,896]{1,0:T(8,128)(2,1)S(1)}, bf16[192,896]{1,0:T(8,128)(2,1)S(1)}, u32[]{:S(2)}, u32[]{:S(2)}) collective-permute-start(bf16[192,896]{1,0:T(8,128)(2,1)S(1)} %slice.48), channel_id=1, source_target_pairs={{0,33},{1,32},{32,1},{33,0},{2,35},{3,34},{34,3},{35,2},{4,37},{5,... | collective-permute-start | bytes 1032200 | tf_op jit(solution)/shard_map/gather/ppermute | solution.py:20
  36.8 10.7 %collective-permute-start.3 = (bf16[192,896]{1,0:T(8,128)(2,1)S(1)}, bf16[192,896]{1,0:T(8,128)(2,1)S(1)}, u32[]{:S(2)}, u32[]{:S(2)}) collective-permute-start(bf16[192,896]{1,0:T(8,128)(2,1)S(1)} %slice.49), channel_id=1, source_target_pairs={{0,1},{1,0},{32,33},{33,32},{2,3},{3,2},{34,35},{35,34},{4,5},{5,4... | collective-permute-start | bytes 1032200 | tf_op jit(solution)/shard_map/gather/ppermute | solution.py:20
  38.7 12.5 %collective-permute-start.9 = (bf16[384,896]{1,0:T(8,128)(2,1)S(1)}, bf16[384,896]{1,0:T(8,128)(2,1)S(1)}, u32[]{:S(2)}, u32[]{:S(2)}) collective-permute-start(bf16[384,896]{1,0:T(8,128)(2,1)S(1)} %collective-permute-done.4.refs_0_), channel_id=1, source_target_pairs={{0,16},{16,0},{1,17},{17,1},{2,18},{18,2},{3,19},{19,3},{4,20},{20... | collective-permute-start | bytes 2064392 | tf_op jit(solution)/shard_map/gather/ppermute | solution.py:29
  38.8 11.9 %collective-permute-start.6 = (bf16[192,896]{1,0:T(8,128)(2,1)S(1)}, bf16[192,896]{1,0:T(8,128)(2,1)}, u32[]{:S(2)}, u32[]{:S(2)}) collective-permute-start(bf16[192,896]{1,0:T(8,128)(2,1)S(1)} %slice.50), channel_id=1, source_target_pairs={{0,64},{64,128},{128,192},{192,0},{1,65},{65,129},{129,193},{193,1... | collective-permute-start | bytes 1032200 | tf_op jit(solution)/shard_map/gather/ppermute | solution.py:25
  40.5 10.4 %collective-permute-start.8 = (bf16[192,896]{1,0:T(8,128)(2,1)S(1)}, bf16[192,896]{1,0:T(8,128)(2,1)}, u32[]{:S(2)}, u32[]{:S(2)}) collective-permute-start(bf16[192,896]{1,0:T(8,128)(2,1)S(1)} %slice.51), channel_id=1, source_target_pairs={{0,192},{64,0},{128,64},{192,128},{1,193},{65,1},{129,65},{193,129... | collective-permute-start | bytes 1032200 | tf_op jit(solution)/shard_map/gather/ppermute | solution.py:25
  47.4 5.8 %collective-permute-start.10 = (bf16[384,896]{1,0:T(8,128)(2,1)S(1)}, bf16[384,896]{1,0:T(8,128)(2,1)S(1)}, u32[]{:S(2)}, u32[]{:S(2)}) collective-permute-start(bf16[384,896]{1,0:T(8,128)(2,1)S(1)} %collective-permute-done.5.refs_1_), channel_id=1, source_target_pairs={{0,16},{16,0},{1,17},{17,1},{2,18},{18,2},{3,19},{19,3},{4,20},{20... | collective-permute-start | bytes 2064392 | tf_op jit(solution)/shard_map/gather/ppermute | solution.py:29
  48.2 5.0 %collective-permute-start.13 = (bf16[384,896]{1,0:T(8,128)(2,1)S(1)}, bf16[384,896]{1,0:T(8,128)(2,1)}, u32[]{:S(2)}, u32[]{:S(2)}) collective-permute-start(bf16[384,896]{1,0:T(8,128)(2,1)S(1)} %collective-permute-done.7.refs_4_), channel_id=1, source_target_pairs={{0,16},{16,0},{1,17},{17,1},{2,18},{18,2},{3,19},{19,3},{4,20},{20... | collective-permute-start | bytes 2064392 | tf_op jit(solution)/shard_map/gather/ppermute | solution.py:29
  70.4 107.8 %all-gather.2.cloned.1.call-start = ((), (), s32[]{:S(2)}) async-start(), calls=%async_computation.2 | async-start | bytes 2654208 | tf_op jit(solution)/shard_map/combined/all_gather | solution.py:138
  183.9 20.0 %collective-permute-start.16 = (bf16[8,24,1792]{2,1,0:T(8,128)(2,1)S(1)}, bf16[8,24,1792]{2,1,0:T(8,128)(2,1)S(1)}, u32[]{:S(2)}, u32[]{:S(2)}) collective-permute-start(bf16[8,24,1792]{2,1,0:T(8,128)(2,1)S(1)} %get-tuple-element.12), channel_id=1, source_target_pairs={{0,32},{1,33},{32,0},{33,1},{2,34},{3,35},{34,2},{35,3},{4,36},{5,... | collective-permute-start | bytes 2064392 | tf_op jit(solution)/shard_map/gamma/ppermute | solution.py:20
  186.9 27.2 %collective-permute-start.15 = (bf16[8,24,1792]{2,1,0:T(8,128)(2,1)S(1)}, bf16[8,24,1792]{2,1,0:T(8,128)(2,1)S(1)}, u32[]{:S(2)}, u32[]{:S(2)}) collective-permute-start(bf16[8,24,1792]{2,1,0:T(8,128)(2,1)S(1)} %get-tuple-element.11), channel_id=1, source_target_pairs={{0,33},{1,32},{32,1},{33,0},{2,35},{3,34},{34,3},{35,2},{4,37},{5,... | collective-permute-start | bytes 2064392 | tf_op jit(solution)/shard_map/gamma/ppermute | solution.py:20
  194.6 19.6 %collective-permute-start.14 = (bf16[8,24,1792]{2,1,0:T(8,128)(2,1)S(1)}, bf16[8,24,1792]{2,1,0:T(8,128)(2,1)S(1)}, u32[]{:S(2)}, u32[]{:S(2)}) collective-permute-start(bf16[8,24,1792]{2,1,0:T(8,128)(2,1)S(1)} %get-tuple-element.10), channel_id=1, source_target_pairs={{0,1},{1,0},{32,33},{33,32},{2,3},{3,2},{34,35},{35,34},{4,5},{5,4... | collective-permute-start | bytes 2064392 | tf_op jit(solution)/shard_map/gamma/ppermute | solution.py:20
  215.9 11.4 %collective-permute-start.17 = (bf16[24,1792]{1,0:T(8,128)(2,1)S(1)}, bf16[24,1792]{1,0:T(8,128)(2,1)S(1)}, u32[]{:S(2)}, u32[]{:S(2)}) collective-permute-start(bf16[24,1792]{1,0:T(8,128)(2,1)S(1)} %get-tuple-element.19), channel_id=1, source_target_pairs={{0,2},{2,4},{4,6},{6,8},{8,10},{10,12},{12,14},{14,0},{1,3},{3,5},... | collective-permute-start | bytes 258056 | tf_op jit(solution)/shard_map/spread/ppermute | solution.py:25
  217.1 11.2 %collective-permute-start.18 = (bf16[24,1792]{1,0:T(8,128)(2,1)S(1)}, bf16[24,1792]{1,0:T(8,128)(2,1)S(1)}, u32[]{:S(2)}, u32[]{:S(2)}) collective-permute-start(bf16[24,1792]{1,0:T(8,128)(2,1)S(1)} %get-tuple-element.18), channel_id=1, source_target_pairs={{0,4},{2,6},{4,8},{6,10},{8,12},{10,14},{12,0},{14,2},{1,5},{3,7},... | collective-permute-start | bytes 258056 | tf_op jit(solution)/shard_map/spread/ppermute | solution.py:25
  219.1 13.7 %collective-permute-start.19 = (bf16[24,1792]{1,0:T(8,128)(2,1)S(1)}, bf16[24,1792]{1,0:T(8,128)(2,1)S(1)}, u32[]{:S(2)}, u32[]{:S(2)}) collective-permute-start(bf16[24,1792]{1,0:T(8,128)(2,1)S(1)} %get-tuple-element.17), channel_id=1, source_target_pairs={{0,6},{2,8},{4,10},{6,12},{8,14},{10,0},{12,2},{14,4},{1,7},{3,9},... | collective-permute-start | bytes 258056 | tf_op jit(solution)/shard_map/spread/ppermute | solution.py:25
  221.4 11.4 %collective-permute-start.20 = (bf16[24,1792]{1,0:T(8,128)(2,1)S(1)}, bf16[24,1792]{1,0:T(8,128)(2,1)S(1)}, u32[]{:S(2)}, u32[]{:S(2)}) collective-permute-start(bf16[24,1792]{1,0:T(8,128)(2,1)S(1)} %get-tuple-element.16), channel_id=1, source_target_pairs={{0,8},{2,10},{4,12},{6,14},{8,0},{10,2},{12,4},{14,6},{1,9},{3,11}... | collective-permute-start | bytes 258056 | tf_op jit(solution)/shard_map/spread/ppermute | solution.py:25
  224.4 13.6 %collective-permute-start.21 = (bf16[24,1792]{1,0:T(8,128)(2,1)S(1)}, bf16[24,1792]{1,0:T(8,128)(2,1)S(1)}, u32[]{:S(2)}, u32[]{:S(2)}) collective-permute-start(bf16[24,1792]{1,0:T(8,128)(2,1)S(1)} %get-tuple-element.15), channel_id=1, source_target_pairs={{0,10},{2,12},{4,14},{6,0},{8,2},{10,4},{12,6},{14,8},{1,11},{3,13... | collective-permute-start | bytes 258056 | tf_op jit(solution)/shard_map/spread/ppermute | solution.py:25
  227.3 11.2 %collective-permute-start.22 = (bf16[24,1792]{1,0:T(8,128)(2,1)S(1)}, bf16[24,1792]{1,0:T(8,128)(2,1)S(1)}, u32[]{:S(2)}, u32[]{:S(2)}) collective-permute-start(bf16[24,1792]{1,0:T(8,128)(2,1)S(1)} %get-tuple-element.14), channel_id=1, source_target_pairs={{0,12},{2,14},{4,0},{6,2},{8,4},{10,6},{12,8},{14,10},{1,13},{3,15... | collective-permute-start | bytes 258056 | tf_op jit(solution)/shard_map/spread/ppermute | solution.py:25
  228.3 12.4 %collective-permute-start.23 = (bf16[24,1792]{1,0:T(8,128)(2,1)S(1)}, bf16[24,1792]{1,0:T(8,128)(2,1)S(1)}, u32[]{:S(2)}, u32[]{:S(2)}) collective-permute-start(bf16[24,1792]{1,0:T(8,128)(2,1)S(1)} %get-tuple-element.13), channel_id=1, source_target_pairs={{0,14},{2,0},{4,2},{6,4},{8,6},{10,8},{12,10},{14,12},{1,15},{3,1}... | collective-permute-start | bytes 258056 | tf_op jit(solution)/shard_map/spread/ppermute | solution.py:25
  (18 other events, 155.7 us)
Sparse Core Ops, SparseCore 0:
  70.5 59.4 reduce-scatter.1
  136.7 41.5 all-gather.1
